TPU v7x, 32 devices: a whole 2x2x4 slice. The times are simulated.
32 devices in a mesh: row: 8 (over z, x), col: 4 (over y, core).
Axes of the slice: x: 2, y: 2, z: 4, core: 2. Of those that a mesh axis runs over, the one named last changes fastest.
Arguments:
- x_points: bfloat16 [8192, 64], P(('row', 'col')), may hold values from -6 to 6
- y_points: bfloat16 [32768, 64], P(('col', 'row')), may hold values from -6 to 6
- row_mass: bfloat16 [8192], P(('row', 'col')), may hold values from 1 to 30, as said below
- col_mass: bfloat16 [32768], P(('col', 'row')), may hold values from 1 to 30, as said below
- multipliers: bfloat16 [8192, 64], P(('row', 'col')), may hold values from -12 to 12
- col_potential: bfloat16 [32768], P(('col', 'row')), may hold values from -3 to 3
- basket: float32 [64], replicated, may hold values from 0.05 to 0.25
- damping: float32 [64], replicated, may hold values from 0.3 to 1.5
Outputs:
- row_potential: float32 [8192], P('row')
- col_potential_new: float32 [32768], P('col')
- multipliers_new: float32 [8192, 64], P(('row', 'col'))
Inputs may be any that keep to these rules, and one draw needn't show every extreme that they name: `row_mass`: weights rise along the points' order by up to a factor of three. `col_mass`: weights rise along the points' order by up to a factor of three.
All inputs are finite; a program needn't handle non-finite values.
Results may differ from a plain program's by a relative error of at most 0.0012.
Values may be sent and summed in bfloat16 or wider, within the bound.
A program may use at most 64 MiB of HBM per device.

v0:
```python
import jax
import jax.numpy as jnp
from jax import lax
from jax.sharding import PartitionSpec as P

EPS = 0.5
KAPPA = 0.5
RIDGE = 1.0


def joined(value, axis, join):
    pieces = jax.tree.map(lambda part: lax.all_gather(part, axis), value)
    head = jax.tree.map(lambda part: part[0], pieces)
    tail = jax.tree.map(lambda part: part[1:], pieces)
    subtotal, _ = lax.scan(lambda subtotal, piece: (join(subtotal, piece), None), head, tail)
    return subtotal


def prepare_rows(x_rows, mult_rows, basket):
    xf = x_rows.astype(jnp.float32)
    hf = mult_rows.astype(jnp.float32)
    width = xf.shape[1]
    query = hf + 2.0 * KAPPA / width * xf
    row_term = -jnp.sum(hf * xf, axis=1) - KAPPA / width * jnp.sum(xf * xf, axis=1)
    row_basket = jnp.sum(xf * basket[None, :], axis=1)
    return (query, row_term, row_basket)


def prepare_cols(y_cols, basket):
    yf = y_cols.astype(jnp.float32)
    width = yf.shape[1]
    col_term = -(KAPPA / width) * jnp.sum(yf * yf, axis=1)
    col_basket = jnp.sum(yf * basket[None, :], axis=1)
    features = jnp.concatenate([yf, yf * yf], axis=1).astype(jnp.bfloat16)
    return (yf, col_term, col_basket, features)


def scores(query, row_term, row_basket, y_float, col_term, col_basket):
    dots = lax.dot_general(
        query,
        y_float,
        (((1,), (1,)), ((), ())),
        precision=lax.Precision.HIGHEST,
        preferred_element_type=jnp.float32,
    )
    payoff = jax.nn.relu(col_basket[None, :] - row_basket[:, None])
    return (dots + row_term[:, None] + col_term[None, :] + payoff) / EPS


def lse_join(first, second):
    top = jnp.maximum(first[0], second[0])
    total = first[1] * jnp.exp(first[0] - top) + second[1] * jnp.exp(second[0] - top)
    return (top, total)


def on_device(x_points, y_points, row_mass, col_mass, multipliers, col_potential, basket, damping):
    x_rows, mult_rows, mass_rows = (
        lax.all_gather(x_points, "col", axis=0, tiled=True),
        lax.all_gather(multipliers, "col", axis=0, tiled=True),
        lax.all_gather(row_mass, "col", axis=0, tiled=True),
    )
    y_cols, pot_cols, mass_cols = (
        lax.all_gather(y_points, "row", axis=0, tiled=True),
        lax.all_gather(col_potential, "row", axis=0, tiled=True),
        lax.all_gather(col_mass, "row", axis=0, tiled=True),
    )
    query, row_term, row_basket = prepare_rows(x_rows, mult_rows, basket)
    y_float, col_term, col_basket, features = prepare_cols(y_cols, basket)
    row_weight = mass_rows.astype(jnp.float32)
    col_weight = mass_cols.astype(jnp.float32)
    log_row = jnp.log(row_weight)
    log_col = jnp.log(col_weight)
    nrows = x_rows.shape[0]
    block = min(128, nrows)
    count = nrows // block
    starts = jnp.arange(count, dtype=jnp.int32) * block

    def cut(arr, start):
        return lax.dynamic_slice_in_dim(arr, start, block, 0)

    def block_scores(start):
        return scores(
            cut(query, start),
            cut(row_term, start),
            cut(row_basket, start),
            y_float,
            col_term,
            col_basket,
        )

    gshift = pot_cols.astype(jnp.float32) / EPS + log_col

    def row_pass(start):
        z = block_scores(start) + gshift[None, :]
        top = jnp.max(z, axis=1)
        total = jnp.sum(jnp.exp(z - top[:, None]), axis=1)
        return (top, total)

    row_tops, row_totals = lax.map(row_pass, starts)
    row_tops = row_tops.reshape(nrows)
    row_totals = row_totals.reshape(nrows)
    mu_total, nu_total = lax.psum(
        (jnp.sum(row_mass.astype(jnp.float32)), jnp.sum(col_mass.astype(jnp.float32))),
        ("row", "col"),
    )
    row_top, row_total = joined((row_tops, row_totals), "col", lse_join)
    log_nu_total = jnp.log(nu_total)
    row_potential = -EPS * (row_top + jnp.log(row_total) - log_nu_total)
    fshift = row_potential / EPS + log_row

    def col_pass(start):
        z = block_scores(start) + cut(fshift, start)[:, None]
        top = jnp.max(z, axis=0)
        total = jnp.sum(jnp.exp(z - top[None, :]), axis=0)
        return (top, total)

    col_tops, col_totals = lax.map(col_pass, starts)
    col_top = jnp.max(col_tops, axis=0)
    col_total = jnp.sum(col_totals * jnp.exp(col_tops - col_top[None, :]), axis=0)
    peak = lax.pmax(col_top, "row")
    scaled = col_total * jnp.exp(col_top - peak)
    whole = lax.psum(scaled, "row")
    col_potential_new = -EPS * (peak + jnp.log(whole) - jnp.log(mu_total))
    gq = col_potential_new / EPS + log_col - log_nu_total
    fq = row_potential / EPS

    def moment_pass(start):
        plan = jnp.exp(block_scores(start) + cut(fq, start)[:, None] + gq[None, :]).astype(
            jnp.bfloat16
        )
        both = jnp.dot(plan, features, preferred_element_type=jnp.float32)
        mass = jnp.sum(plan.astype(jnp.float32), axis=1)
        return (both, mass)

    both, mass = lax.map(moment_pass, starts)
    both = both.reshape(nrows, features.shape[1])
    mass = mass.reshape(nrows)
    share = x_points.shape[0]
    both_all, mass_all = lax.psum((both, mass), "col")
    offset = lax.axis_index("col") * share
    own_both = lax.dynamic_slice_in_dim(both_all, offset, share, 0)
    own_mass = lax.dynamic_slice_in_dim(mass_all, offset, share, 0)
    width = x_points.shape[1]
    first = own_both[:, :width]
    second = own_both[:, width:]
    xf = x_points.astype(jnp.float32)
    grad = first - xf * own_mass[:, None]
    curv = (second - 2.0 * xf * first + xf * xf * own_mass[:, None]) / EPS + RIDGE
    multipliers_new = multipliers.astype(jnp.float32) - damping[None, :] * grad / curv
    return (row_potential, col_potential_new, multipliers_new)


def solution(mesh):
    placed = (
        P(("row", "col"), None),
        P(("col", "row"), None),
        P(("row", "col")),
        P(("col", "row")),
        P(("row", "col"), None),
        P(("col", "row")),
        P(),
        P(),
    )
    return jax.shard_map(
        on_device,
        mesh=mesh,
        in_specs=placed,
        out_specs=(P("row"), P("col"), P(("row", "col"), None)),
        check_vma=False,
    )
```

profile of v0, /device:TPU:0, one launch (start us, length us, event | category | flops | bytes accessed | tf_op | source)
XLA Modules:
  0.0 507.5 jit_solution(7719395594893005991)
XLA Ops:
  11.6 43.1 %all-reduce = (f32[]{:T(128)}, f32[]{:T(128)}) all-reduce(f32[]{:T(128)} %convert_reduce_fusion.1, f32[]{:T(128)} %convert_reduce_fusion.2), channel_id=1, replica_groups=mesh['row'=8,'col'=4] {'row','col'}, use_global_device_ids=true, to_apply=%region_12.13 | all-reduce | flops 2 | bytes 16 | tf_op jit(solution)/shard_map/psum | solution.py:102
  63.9 26.1 %all_gather.28 = bf16[8192]{0:T(1024)(128)(2,1)S(1)} all-gather(bf16[1024]{0:T(1024)(128)(2,1)} %param.19), channel_id=1, replica_groups=mesh['row'=8,'col'=4] {'row'}, dimensions={0}, use_global_device_ids=true | all-gather | bytes 18432 | tf_op jit(solution)/shard_map/all_gather | solution.py:65
  90.0 26.1 %all_gather.27 = bf16[8192]{0:T(1024)(128)(2,1)S(1)} all-gather(bf16[1024]{0:T(1024)(128)(2,1)} %param.21), channel_id=1, replica_groups=mesh['row'=8,'col'=4] {'row'}, dimensions={0}, use_global_device_ids=true | all-gather | bytes 18432 | tf_op jit(solution)/shard_map/all_gather | solution.py:64
  137.0 80.1 %while.48 = (s32[]{:T(128)}, f32[8,128]{1,0:T(8,128)S(1)}, f32[8,128]{1,0:T(8,128)S(1)}, s32[8]{0:T(128)S(1)}, f32[1024,64]{1,0:T(8,128)S(1)}, /*index=5*/f32[81...) while((s32[]{:T(128)}, f32[8,128]{1,0:T(8,128)S(1)}, ...), condition=%wide.region_8.9_spmd, body=%wide.region_5.8_spmd.sunk | while | flops 815791872 | bytes 10656463 | solution.py:99
  139.7 6.5 %fusion.53 = (f32[128]{0:T(128)S(1)}, f32[128,8192]{1,0:T(8,128)S(1)}) fusion(f32[8192]{0:T(1024)S(1)} %get-tuple-element.629, f32[128]{0:T(128)S(1)} %dynamic_slice.89, f32[8192]{0:T(1024)S(1)} %get-tuple-element.627, f32[8192]{0:T(1024)S(1)} %get-tuple-element.626, f32[128]{0:T(128)S(1)} %dynamic_slice.90, f32[8192,64]{1,0:T(8,128)} %get-tuple-element.624, ...), kind=kOutput, calls=%fused_computation.76.clone.1 | convolution fusion | flops 813694848 | bytes 6456836 | tf_op jit(solution)/shard_map/while/body/eval_jaxpr/dot_general | solution.py:39
  149.7 6.5 %fusion.53 = (f32[128]{0:T(128)S(1)}, f32[128,8192]{1,0:T(8,128)S(1)}) fusion(f32[8192]{0:T(1024)S(1)} %get-tuple-element.629, f32[128]{0:T(128)S(1)} %dynamic_slice.89, f32[8192]{0:T(1024)S(1)} %get-tuple-element.627, f32[8192]{0:T(1024)S(1)} %get-tuple-element.626, f32[128]{0:T(128)S(1)} %dynamic_slice.90, f32[8192,64]{1,0:T(8,128)} %get-tuple-element.624, ...), kind=kOutput, calls=%fused_computation.76.clone.1 | convolution fusion | flops 813694848 | bytes 6456836 | tf_op jit(solution)/shard_map/while/body/eval_jaxpr/dot_general | solution.py:39
  159.7 6.5 %fusion.53 = (f32[128]{0:T(128)S(1)}, f32[128,8192]{1,0:T(8,128)S(1)}) fusion(f32[8192]{0:T(1024)S(1)} %get-tuple-element.629, f32[128]{0:T(128)S(1)} %dynamic_slice.89, f32[8192]{0:T(1024)S(1)} %get-tuple-element.627, f32[8192]{0:T(1024)S(1)} %get-tuple-element.626, f32[128]{0:T(128)S(1)} %dynamic_slice.90, f32[8192,64]{1,0:T(8,128)} %get-tuple-element.624, ...), kind=kOutput, calls=%fused_computation.76.clone.1 | convolution fusion | flops 813694848 | bytes 6456836 | tf_op jit(solution)/shard_map/while/body/eval_jaxpr/dot_general | solution.py:39
  169.7 6.5 %fusion.53 = (f32[128]{0:T(128)S(1)}, f32[128,8192]{1,0:T(8,128)S(1)}) fusion(f32[8192]{0:T(1024)S(1)} %get-tuple-element.629, f32[128]{0:T(128)S(1)} %dynamic_slice.89, f32[8192]{0:T(1024)S(1)} %get-tuple-element.627, f32[8192]{0:T(1024)S(1)} %get-tuple-element.626, f32[128]{0:T(128)S(1)} %dynamic_slice.90, f32[8192,64]{1,0:T(8,128)} %get-tuple-element.624, ...), kind=kOutput, calls=%fused_computation.76.clone.1 | convolution fusion | flops 813694848 | bytes 6456836 | tf_op jit(solution)/shard_map/while/body/eval_jaxpr/dot_general | solution.py:39
  179.7 6.5 %fusion.53 = (f32[128]{0:T(128)S(1)}, f32[128,8192]{1,0:T(8,128)S(1)}) fusion(f32[8192]{0:T(1024)S(1)} %get-tuple-element.629, f32[128]{0:T(128)S(1)} %dynamic_slice.89, f32[8192]{0:T(1024)S(1)} %get-tuple-element.627, f32[8192]{0:T(1024)S(1)} %get-tuple-element.626, f32[128]{0:T(128)S(1)} %dynamic_slice.90, f32[8192,64]{1,0:T(8,128)} %get-tuple-element.624, ...), kind=kOutput, calls=%fused_computation.76.clone.1 | convolution fusion | flops 813694848 | bytes 6456836 | tf_op jit(solution)/shard_map/while/body/eval_jaxpr/dot_general | solution.py:39
  189.7 6.5 %fusion.53 = (f32[128]{0:T(128)S(1)}, f32[128,8192]{1,0:T(8,128)S(1)}) fusion(f32[8192]{0:T(1024)S(1)} %get-tuple-element.629, f32[128]{0:T(128)S(1)} %dynamic_slice.89, f32[8192]{0:T(1024)S(1)} %get-tuple-element.627, f32[8192]{0:T(1024)S(1)} %get-tuple-element.626, f32[128]{0:T(128)S(1)} %dynamic_slice.90, f32[8192,64]{1,0:T(8,128)} %get-tuple-element.624, ...), kind=kOutput, calls=%fused_computation.76.clone.1 | convolution fusion | flops 813694848 | bytes 6456836 | tf_op jit(solution)/shard_map/while/body/eval_jaxpr/dot_general | solution.py:39
  199.7 6.5 %fusion.53 = (f32[128]{0:T(128)S(1)}, f32[128,8192]{1,0:T(8,128)S(1)}) fusion(f32[8192]{0:T(1024)S(1)} %get-tuple-element.629, f32[128]{0:T(128)S(1)} %dynamic_slice.89, f32[8192]{0:T(1024)S(1)} %get-tuple-element.627, f32[8192]{0:T(1024)S(1)} %get-tuple-element.626, f32[128]{0:T(128)S(1)} %dynamic_slice.90, f32[8192,64]{1,0:T(8,128)} %get-tuple-element.624, ...), kind=kOutput, calls=%fused_computation.76.clone.1 | convolution fusion | flops 813694848 | bytes 6456836 | tf_op jit(solution)/shard_map/while/body/eval_jaxpr/dot_general | solution.py:39
  209.7 6.5 %fusion.53 = (f32[128]{0:T(128)S(1)}, f32[128,8192]{1,0:T(8,128)S(1)}) fusion(f32[8192]{0:T(1024)S(1)} %get-tuple-element.629, f32[128]{0:T(128)S(1)} %dynamic_slice.89, f32[8192]{0:T(1024)S(1)} %get-tuple-element.627, f32[8192]{0:T(1024)S(1)} %get-tuple-element.626, f32[128]{0:T(128)S(1)} %dynamic_slice.90, f32[8192,64]{1,0:T(8,128)} %get-tuple-element.624, ...), kind=kOutput, calls=%fused_computation.76.clone.1 | convolution fusion | flops 813694848 | bytes 6456836 | tf_op jit(solution)/shard_map/while/body/eval_jaxpr/dot_general | solution.py:39
  228.4 80.8 %while.50 = (s32[]{:T(128)}, f32[8,8192]{1,0:T(8,128)S(1)}, f32[8,8192]{1,0:T(8,128)S(1)}, s32[8]{0:T(128)S(1)}, f32[1024,64]{1,0:T(8,128)S(1)}, /*index=5*/f32[...) while((s32[]{:T(128)}, f32[8,8192]{1,0:T(8,128)S(1)}, ...), condition=%wide.region_16.17_spmd, body=%wide.region_13.16_spmd.sunk | while | flops 815775744 | bytes 10851027 | solution.py:117
  231.2 6.4 %fusion.55 = (f32[8192]{0:T(1024)S(1)}, f32[128,8192]{1,0:T(8,128)S(1)}) fusion(f32[128]{0:T(128)S(1)} %dynamic_slice.94, f32[128]{0:T(128)S(1)} %dynamic_slice.95, f32[8192]{0:T(1024)S(1)} %get-tuple-element.687, f32[8192]{0:T(1024)S(1)} %get-tuple-element.686, f32[128]{0:T(128)S(1)} %dynamic_slice.96, f32[8192,64]{1,0:T(8,128)} %get-tuple-element.684, ...), kind=kOutput, calls=%fused_computation.77.clone.1 | convolution fusion | flops 813686784 | bytes 6456836 | tf_op jit(solution)/shard_map/while/body/eval_jaxpr/dot_general | solution.py:39
  241.3 6.4 %fusion.55 = (f32[8192]{0:T(1024)S(1)}, f32[128,8192]{1,0:T(8,128)S(1)}) fusion(f32[128]{0:T(128)S(1)} %dynamic_slice.94, f32[128]{0:T(128)S(1)} %dynamic_slice.95, f32[8192]{0:T(1024)S(1)} %get-tuple-element.687, f32[8192]{0:T(1024)S(1)} %get-tuple-element.686, f32[128]{0:T(128)S(1)} %dynamic_slice.96, f32[8192,64]{1,0:T(8,128)} %get-tuple-element.684, ...), kind=kOutput, calls=%fused_computation.77.clone.1 | convolution fusion | flops 813686784 | bytes 6456836 | tf_op jit(solution)/shard_map/while/body/eval_jaxpr/dot_general | solution.py:39
  251.4 6.4 %fusion.55 = (f32[8192]{0:T(1024)S(1)}, f32[128,8192]{1,0:T(8,128)S(1)}) fusion(f32[128]{0:T(128)S(1)} %dynamic_slice.94, f32[128]{0:T(128)S(1)} %dynamic_slice.95, f32[8192]{0:T(1024)S(1)} %get-tuple-element.687, f32[8192]{0:T(1024)S(1)} %get-tuple-element.686, f32[128]{0:T(128)S(1)} %dynamic_slice.96, f32[8192,64]{1,0:T(8,128)} %get-tuple-element.684, ...), kind=kOutput, calls=%fused_computation.77.clone.1 | convolution fusion | flops 813686784 | bytes 6456836 | tf_op jit(solution)/shard_map/while/body/eval_jaxpr/dot_general | solution.py:39
  261.5 6.4 %fusion.55 = (f32[8192]{0:T(1024)S(1)}, f32[128,8192]{1,0:T(8,128)S(1)}) fusion(f32[128]{0:T(128)S(1)} %dynamic_slice.94, f32[128]{0:T(128)S(1)} %dynamic_slice.95, f32[8192]{0:T(1024)S(1)} %get-tuple-element.687, f32[8192]{0:T(1024)S(1)} %get-tuple-element.686, f32[128]{0:T(128)S(1)} %dynamic_slice.96, f32[8192,64]{1,0:T(8,128)} %get-tuple-element.684, ...), kind=kOutput, calls=%fused_computation.77.clone.1 | convolution fusion | flops 813686784 | bytes 6456836 | tf_op jit(solution)/shard_map/while/body/eval_jaxpr/dot_general | solution.py:39
  271.6 6.4 %fusion.55 = (f32[8192]{0:T(1024)S(1)}, f32[128,8192]{1,0:T(8,128)S(1)}) fusion(f32[128]{0:T(128)S(1)} %dynamic_slice.94, f32[128]{0:T(128)S(1)} %dynamic_slice.95, f32[8192]{0:T(1024)S(1)} %get-tuple-element.687, f32[8192]{0:T(1024)S(1)} %get-tuple-element.686, f32[128]{0:T(128)S(1)} %dynamic_slice.96, f32[8192,64]{1,0:T(8,128)} %get-tuple-element.684, ...), kind=kOutput, calls=%fused_computation.77.clone.1 | convolution fusion | flops 813686784 | bytes 6456836 | tf_op jit(solution)/shard_map/while/body/eval_jaxpr/dot_general | solution.py:39
  281.7 6.4 %fusion.55 = (f32[8192]{0:T(1024)S(1)}, f32[128,8192]{1,0:T(8,128)S(1)}) fusion(f32[128]{0:T(128)S(1)} %dynamic_slice.94, f32[128]{0:T(128)S(1)} %dynamic_slice.95, f32[8192]{0:T(1024)S(1)} %get-tuple-element.687, f32[8192]{0:T(1024)S(1)} %get-tuple-element.686, f32[128]{0:T(128)S(1)} %dynamic_slice.96, f32[8192,64]{1,0:T(8,128)} %get-tuple-element.684, ...), kind=kOutput, calls=%fused_computation.77.clone.1 | convolution fusion | flops 813686784 | bytes 6456836 | tf_op jit(solution)/shard_map/while/body/eval_jaxpr/dot_general | solution.py:39
  291.8 6.4 %fusion.55 = (f32[8192]{0:T(1024)S(1)}, f32[128,8192]{1,0:T(8,128)S(1)}) fusion(f32[128]{0:T(128)S(1)} %dynamic_slice.94, f32[128]{0:T(128)S(1)} %dynamic_slice.95, f32[8192]{0:T(1024)S(1)} %get-tuple-element.687, f32[8192]{0:T(1024)S(1)} %get-tuple-element.686, f32[128]{0:T(128)S(1)} %dynamic_slice.96, f32[8192,64]{1,0:T(8,128)} %get-tuple-element.684, ...), kind=kOutput, calls=%fused_computation.77.clone.1 | convolution fusion | flops 813686784 | bytes 6456836 | tf_op jit(solution)/shard_map/while/body/eval_jaxpr/dot_general | solution.py:39
  309.3 33.0 %pmax.7 = f32[8192]{0:T(1024)S(1)} all-reduce(f32[8192]{0:T(1024)S(1)} %reduce_max.27), channel_id=1, replica_groups=mesh['row'=8,'col'=4] {'row'}, use_global_device_ids=true, to_apply=%region_18.19 | all-reduce | flops 8192 | bytes 65536 | tf_op jit(solution)/shard_map/pmax | solution.py:120
  342.5 33.0 %psum.36 = f32[8192]{0:T(1024)S(1)} all-reduce(f32[8192]{0:T(1024)S(1)} %exponential_multiply_fusion), channel_id=1, replica_groups=mesh['row'=8,'col'=4] {'row'}, use_global_device_ids=true, to_apply=%region_20.21 | all-reduce | flops 8192 | bytes 65536 | tf_op jit(solution)/shard_map/psum | solution.py:122
  379.5 87.9 %while.51 = (s32[]{:T(128)}, f32[8,128,128]{2,1,0:T(8,128)S(1)}, f32[8,128]{1,0:T(8,128)S(1)}, s32[8]{0:T(128)S(1)}, f32[1024,64]{1,0:T(8,128)S(1)}, /*index=5*/...) while((s32[]{:T(128)}, f32[8,128,128]{2,1,0:T(8,128)S(1)}, ...), condition=%wide.region_25.26_spmd, body=%wide.region_23.25_spmd.sunk | while | flops 1085276032 | bytes 8624355 | solution.py:135
  382.3 7.5 %convert_reduce_fusion.4 = (f32[128]{0:T(128)S(1)}, bf16[128,8192]{1,0:T(8,128)(2,1)S(1)}) fusion(f32[8192]{0:T(1024)S(1)} %get-tuple-element.736, f32[128]{0:T(128)S(1)} %dynamic_slice.99, f32[128]{0:T(128)S(1)} %dynamic_slice.100, f32[8192]{0:T(1024)S(1)} %get-tuple-element.733, f32[8192]{0:T(1024)S(1)} %get-tuple-element.732, ...), kind=kOutput, calls=%fused_computation.27.clone.1 | convolution fusion | flops 816840576 | bytes 4360196 | tf_op jit(solution)/shard_map/while/body/eval_jaxpr/dot_general | solution.py:39
  393.3 7.5 %convert_reduce_fusion.4 = (f32[128]{0:T(128)S(1)}, bf16[128,8192]{1,0:T(8,128)(2,1)S(1)}) fusion(f32[8192]{0:T(1024)S(1)} %get-tuple-element.736, f32[128]{0:T(128)S(1)} %dynamic_slice.99, f32[128]{0:T(128)S(1)} %dynamic_slice.100, f32[8192]{0:T(1024)S(1)} %get-tuple-element.733, f32[8192]{0:T(1024)S(1)} %get-tuple-element.732, ...), kind=kOutput, calls=%fused_computation.27.clone.1 | convolution fusion | flops 816840576 | bytes 4360196 | tf_op jit(solution)/shard_map/while/body/eval_jaxpr/dot_general | solution.py:39
  404.3 7.5 %convert_reduce_fusion.4 = (f32[128]{0:T(128)S(1)}, bf16[128,8192]{1,0:T(8,128)(2,1)S(1)}) fusion(f32[8192]{0:T(1024)S(1)} %get-tuple-element.736, f32[128]{0:T(128)S(1)} %dynamic_slice.99, f32[128]{0:T(128)S(1)} %dynamic_slice.100, f32[8192]{0:T(1024)S(1)} %get-tuple-element.733, f32[8192]{0:T(1024)S(1)} %get-tuple-element.732, ...), kind=kOutput, calls=%fused_computation.27.clone.1 | convolution fusion | flops 816840576 | bytes 4360196 | tf_op jit(solution)/shard_map/while/body/eval_jaxpr/dot_general | solution.py:39
  415.3 7.5 %convert_reduce_fusion.4 = (f32[128]{0:T(128)S(1)}, bf16[128,8192]{1,0:T(8,128)(2,1)S(1)}) fusion(f32[8192]{0:T(1024)S(1)} %get-tuple-element.736, f32[128]{0:T(128)S(1)} %dynamic_slice.99, f32[128]{0:T(128)S(1)} %dynamic_slice.100, f32[8192]{0:T(1024)S(1)} %get-tuple-element.733, f32[8192]{0:T(1024)S(1)} %get-tuple-element.732, ...), kind=kOutput, calls=%fused_computation.27.clone.1 | convolution fusion | flops 816840576 | bytes 4360196 | tf_op jit(solution)/shard_map/while/body/eval_jaxpr/dot_general | solution.py:39
  426.2 7.5 %convert_reduce_fusion.4 = (f32[128]{0:T(128)S(1)}, bf16[128,8192]{1,0:T(8,128)(2,1)S(1)}) fusion(f32[8192]{0:T(1024)S(1)} %get-tuple-element.736, f32[128]{0:T(128)S(1)} %dynamic_slice.99, f32[128]{0:T(128)S(1)} %dynamic_slice.100, f32[8192]{0:T(1024)S(1)} %get-tuple-element.733, f32[8192]{0:T(1024)S(1)} %get-tuple-element.732, ...), kind=kOutput, calls=%fused_computation.27.clone.1 | convolution fusion | flops 816840576 | bytes 4360196 | tf_op jit(solution)/shard_map/while/body/eval_jaxpr/dot_general | solution.py:39
  437.2 7.5 %convert_reduce_fusion.4 = (f32[128]{0:T(128)S(1)}, bf16[128,8192]{1,0:T(8,128)(2,1)S(1)}) fusion(f32[8192]{0:T(1024)S(1)} %get-tuple-element.736, f32[128]{0:T(128)S(1)} %dynamic_slice.99, f32[128]{0:T(128)S(1)} %dynamic_slice.100, f32[8192]{0:T(1024)S(1)} %get-tuple-element.733, f32[8192]{0:T(1024)S(1)} %get-tuple-element.732, ...), kind=kOutput, calls=%fused_computation.27.clone.1 | convolution fusion | flops 816840576 | bytes 4360196 | tf_op jit(solution)/shard_map/while/body/eval_jaxpr/dot_general | solution.py:39
  448.2 7.5 %convert_reduce_fusion.4 = (f32[128]{0:T(128)S(1)}, bf16[128,8192]{1,0:T(8,128)(2,1)S(1)}) fusion(f32[8192]{0:T(1024)S(1)} %get-tuple-element.736, f32[128]{0:T(128)S(1)} %dynamic_slice.99, f32[128]{0:T(128)S(1)} %dynamic_slice.100, f32[8192]{0:T(1024)S(1)} %get-tuple-element.733, f32[8192]{0:T(1024)S(1)} %get-tuple-element.732, ...), kind=kOutput, calls=%fused_computation.27.clone.1 | convolution fusion | flops 816840576 | bytes 4360196 | tf_op jit(solution)/shard_map/while/body/eval_jaxpr/dot_general | solution.py:39
  459.2 7.5 %convert_reduce_fusion.4 = (f32[128]{0:T(128)S(1)}, bf16[128,8192]{1,0:T(8,128)(2,1)S(1)}) fusion(f32[8192]{0:T(1024)S(1)} %get-tuple-element.736, f32[128]{0:T(128)S(1)} %dynamic_slice.99, f32[128]{0:T(128)S(1)} %dynamic_slice.100, f32[8192]{0:T(1024)S(1)} %get-tuple-element.733, f32[8192]{0:T(1024)S(1)} %get-tuple-element.732, ...), kind=kOutput, calls=%fused_computation.27.clone.1 | convolution fusion | flops 816840576 | bytes 4360196 | tf_op jit(solution)/shard_map/while/body/eval_jaxpr/dot_general | solution.py:39
  474.2 24.9 %all-reduce.3.cloned.1.call-done = f32[1024,128]{0,1:T(8,128)} async-done(((f32[1024,128]{0,1:T(8,128)}), f32[1024,128]{0,1:T(8,128)}) %all-reduce.3.cloned.1.call-update) | async-done | bytes 524304 | tf_op jit(solution)/shard_map/psum | solution.py:139
  (214 shorter events, 102.1 us)
Async XLA Ops:
  7.2 122.4 %all-gather.5.cloned.1.call-start = ((), (), s32[]{:S(2)}) async-start(), calls=%async_computation | async-start | bytes 2359296 | tf_op jit(solution)/shard_map/all_gather | solution.py:63
  9.0 490.1 %all-reduce.3.cloned.1.call-start = ((), (), s32[]{:S(2)}) async-start(), calls=%async_computation.1 | async-start | bytes 1048576 | tf_op jit(solution)/shard_map/psum | solution.py:139
  129.6 5.2 %copy-start = (bf16[8192,64]{1,0:T(8,128)(2,1)S(1)}, bf16[8192,64]{1,0:T(8,128)(2,1)}, u32[]{:S(2)}) copy-start(bf16[8192,64]{1,0:T(8,128)(2,1)} %all-gather.5.cloned.1.call-done) | copy-start | bytes 3145732
  379.5 119.6 %copy-start.1 = (bf16[256,64]{0,1:T(8,128)(2,1)S(1)}, bf16[256,64]{0,1:T(8,128)(2,1)}, u32[]{:S(2)}) copy-start(bf16[256,64]{0,1:T(8,128)(2,1)} %param.16) | copy-start | bytes 98308
  379.5 119.6 %copy-start.2 = (bf16[256,64]{0,1:T(8,128)(2,1)S(1)}, bf16[256,64]{0,1:T(8,128)(2,1)}, u32[]{:S(2)}) copy-start(bf16[256,64]{0,1:T(8,128)(2,1)} %param.20) | copy-start | bytes 98308
  379.5 119.6 %copy-start.3 = (f32[64]{0:T(128)S(1)}, f32[64]{0:T(128)}, u32[]{:S(2)}) copy-start(f32[64]{0:T(128)} %param.23) | copy-start | bytes 772
Sparse Core Ops, SparseCore 0:
  10.1 52.9 all-gather.4
  468.6 30.4 all-reduce.2
where the time goes:
time: 509 us; the launch traced here: 508 us
  blocking collectives  195 us (38%)
  matrix products  168 us (33%)
  loops' own time  47.4 us (9%)
  other arithmetic  28.6 us (6%)
  local copies, waits for them, and re-layouts  27.5 us (5%)
  waiting for transfers between devices  24.9 us (5%)
  between operations  15.6 us (3%)
    dot_general x24, matrix products, scores(): lax.dot_general(query, y_float, (((1,), (1,)), ((), ())), precision=lax.P...  163 us
    psum x1, blocking collectives, on_device(): lax.psum((jnp.sum(row_mass.astype(jnp.float32)), jnp.sum(col_mass.astype(...  43.1 us
    pmax x1, blocking collectives, on_device(): peak = lax.pmax(col_top, 'row')  33 us
    psum x1, blocking collectives, on_device(): whole = lax.psum(scaled, 'row')  33 us
    all_gather x1, blocking collectives, on_device(): lax.all_gather(col_potential, 'row', axis=0, tiled=True)  26.1 us
    all_gather x1, blocking collectives, on_device(): lax.all_gather(col_mass, 'row', axis=0, tiled=True)  26.1 us
    psum x1, waiting for transfers between devices, on_device(): both_all, mass_all = lax.psum((both, mass), 'col')  24.9 us
    another operation x1, loops' own time, on_device(): col_tops, col_totals = lax.map(col_pass, starts)  15.8 us
  transfers between devices with their start and end apart: 2, of which 1 were waited for; matrix products, arithmetic and copies ran while one was open for 1% of the time, Pallas kernels for 0%

commit v1 on v0

v1 whole, which is shorter than its diff:
```python
import functools
import math
import jax
import jax.numpy as jnp
from jax import lax
from jax.experimental import pallas as pl
from jax.experimental.pallas import tpu as pltpu
from jax.sharding import PartitionSpec as P

EPS = 0.5
KAPPA = 0.5
RIDGE = 1.0
L2E = math.log2(math.e)
LN2 = math.log(2.0)
SCALE = L2E / EPS
LOW = -1e30
F32 = jnp.float32
BF16 = jnp.bfloat16


def split3(value):
    one = value.astype(BF16).astype(F32)
    rest = value - one
    two = rest.astype(BF16).astype(F32)
    return one, two, rest - two


def log2(value):
    return jnp.log(value) * L2E


def kernel(
    nrow, ncol,
    xm_ref, rmass_ref, yt_ref, cinfo_ref, basket_ref, damping_ref,
    rowpot_ref, colpot_ref, mult_ref,
    xbuf, rbuf, ybuf, cbuf, rowmsg, colout, colmsg, cpbuf, gout, gbuf, mout, mbuf,
    q_s, q3_s, rt_s, rb_s, y_s, ft_s, cb_s, ct_s, top_s, sum_s, z_s, plan_s, g_s, f_s,
    xsend, xrecv, rsend, rrecv, zsend, wsend, yrecv, czsend, cwsend, crecv,
    rmsend, rmrecv, cmsend, cmrecv, cpsend, cprecv, gsend, grecv, msend, mrecv,
):
    r = lax.axis_index("row")
    c = lax.axis_index("col")
    xs = xm_ref.shape[0]
    cb = yt_ref.shape[1]
    width = yt_ref.shape[0]
    rows = xs * ncol
    half = nrow // 2
    pair = r % 2
    group = r // 2
    twin = r + 1 - 2 * pair

    def to_col(src, dst, send, recv, other):
        return pltpu.make_async_remote_copy(
            src_ref=src, dst_ref=dst, send_sem=send, recv_sem=recv,
            device_id=(r, other), device_id_type=pl.DeviceIdType.MESH)

    def to_row(src, dst, send, recv, other):
        return pltpu.make_async_remote_copy(
            src_ref=src, dst_ref=dst, send_sem=send, recv_sem=recv,
            device_id=(other, c), device_id_type=pl.DeviceIdType.MESH)

    barrier = pltpu.get_barrier_semaphore()

    @pl.loop(1, ncol)
    def _(k):
        pl.semaphore_signal(barrier, inc=1, device_id=(r, (c + k) % ncol),
                            device_id_type=pl.DeviceIdType.MESH)

    @pl.loop(1, nrow)
    def _(k):
        pl.semaphore_signal(barrier, inc=1, device_id=((r + k) % nrow, c),
                            device_id_type=pl.DeviceIdType.MESH)

    xbuf[c] = xm_ref[...]
    rbuf[c] = rmass_ref[...]
    ybuf[r] = yt_ref[...]
    cbuf[r] = cinfo_ref[...]
    pl.semaphore_wait(barrier, nrow + ncol - 2)

    def x_copy(k, owner):
        return to_col(xbuf.at[owner], xbuf.at[owner], xsend.at[k], xrecv.at[owner],
                      (c + k) % ncol)

    def r_copy(k, owner):
        return to_col(rbuf.at[owner], rbuf.at[owner], rsend.at[k], rrecv.at[owner],
                      (c + k) % ncol)

    @pl.loop(1, ncol)
    def _(k):
        x_copy(k, c).start()
        r_copy(k, c).start()

    def same(k):
        return ((group + half - k) % half) * 2 + pair

    def other(k):
        return ((group + half - k) % half) * 2 + 1 - pair

    def z_copies(k, block):
        goal = ((group + k) % half) * 2 + pair
        return (to_row(cbuf.at[block], cbuf.at[block], czsend.at[k], crecv.at[block], goal),
                to_row(ybuf.at[block], ybuf.at[block], zsend.at[k], yrecv.at[block], goal))

    def w_copies(k, block):
        return (to_row(cbuf.at[block], cbuf.at[block], cwsend.at[k], crecv.at[block], twin),
                to_row(ybuf.at[block], ybuf.at[block], wsend.at[k], yrecv.at[block], twin))

    for copy in w_copies(0, r):
        copy.start()

    @pl.loop(1, half)
    def _(k):
        for copy in z_copies(k, r):
            copy.start()

    top_s[...] = jnp.full(top_s.shape, LOW, F32)
    sum_s[...] = jnp.zeros(sum_s.shape, F32)

    def prepare_block(b):
        y16 = ybuf[b]
        yf = y16.astype(F32)
        sq = yf * yf
        y_s[b, 0:width] = y16
        y_s[b, width:2 * width] = y16
        y_s[b, 2 * width:3 * width] = y16
        y_s[b, 3 * width:4 * width] = jnp.zeros((width, cb), BF16)
        ft_s[b, 0:width] = y16
        ft_s[b, width:2 * width] = sq.astype(BF16)
        ones = lax.broadcasted_iota(jnp.int32, (2 * width, cb), 0) == 0
        ft_s[b, 2 * width:4 * width] = jnp.where(ones, 1.0, 0.0).astype(BF16)
        ct_s[b] = -(SCALE * KAPPA / width) * jnp.sum(sq, axis=0, keepdims=True)
        basket = SCALE * jnp.sum(yf * basket_ref[1][0:width, 0:1], axis=0, keepdims=True)
        cb_s[b] = jnp.broadcast_to(basket, (8, cb))

    def put_cols(b, value):
        row = lax.broadcasted_iota(jnp.int32, (16, cb), 0)
        one, two, three = split3(value)
        ext = jnp.where(row < 3, 1.0, 0.0)
        ext = jnp.where(row == 3, one, ext)
        ext = jnp.where(row == 4, two, ext)
        ext = jnp.where(row == 5, three, ext)
        y_s[b, 3 * width:3 * width + 16] = ext.astype(BF16)

    def put_rows(start, size, value):
        lane = lax.broadcasted_iota(jnp.int32, (size, 128), 1)
        one, two, three = split3(value)
        ext = jnp.where((lane >= 67) & (lane < 70), 1.0, q3_s[pl.ds(start, size)])
        ext = jnp.where(lane == 64, one, ext)
        ext = jnp.where(lane == 65, two, ext)
        ext = jnp.where(lane == 66, three, ext)
        q_s[pl.ds(start, size), 128:256] = ext.astype(BF16)

    prepare_block(r)

    @pl.loop(1, ncol)
    def _(k):
        owner = (c + ncol - k) % ncol
        x_copy(k, owner).wait_recv()
        r_copy(k, owner).wait_recv()

    @pl.loop(0, ncol)
    def _(k):
        both = xbuf[k].astype(F32)
        x = both[:, 0:128]
        h = both[:, 128:256]
        lane = lax.broadcasted_iota(jnp.int32, (xs, 128), 1)
        one, two, three = split3(SCALE * (h + (2.0 * KAPPA / width) * x))
        here = pl.ds(k * xs, xs)
        xb = x * basket_ref[0][0:1, :]
        q_s[here, 0:128] = jnp.where(lane < 64, one, two).astype(BF16)
        q3_s[here] = jnp.where(lane < 64, three, 0.0)
        term = -0.5 * (h * x + (KAPPA / width) * (x * x)) - xb
        rt = jnp.broadcast_to(SCALE * jnp.sum(term, axis=1, keepdims=True), (xs, 128))
        rb_s[here] = jnp.broadcast_to(SCALE * jnp.sum(xb, axis=1, keepdims=True), (xs, 128))
        rt_s[here] = rt
        put_rows(k * xs, xs, rt)

    chunk = min(256, rows)
    tiles = cb // 128

    def dots(b):
        for start in range(0, rows, chunk):
            z_s[start:start + chunk] = jnp.dot(
                q_s[start:start + chunk], y_s[b], preferred_element_type=F32)

    def row_block(b):
        put_cols(b, ct_s[b] + cbuf[b, 0:1])
        dots(b)
        size = 32

        def step(i, _):
            here = pl.ds(pl.multiple_of(i * size, size), size)
            rb = rb_s[here]
            vals = []
            for t in range(tiles):
                span = slice(t * 128, (t + 1) * 128)
                vals.append(z_s[here, span] + jnp.maximum(cb_s[b, 0:1, span], rb))
            old = top_s[here]
            top = functools.reduce(jnp.maximum, vals, old)
            total = sum_s[here] * jnp.exp2(old - top)
            for val in vals:
                total = total + jnp.exp2(val - top)
            top_s[here] = top
            sum_s[here] = total
            return 0

        lax.fori_loop(0, rows // size, step, 0, unroll=True)

    @pl.loop(0, half)
    def _(k):
        first = same(k)

        @pl.when(k > 0)
        def _():
            for copy in z_copies(k, first):
                copy.wait_recv()
            for copy in w_copies(k, first):
                copy.start()
            prepare_block(first)

        row_block(first)
        second = other(k)
        for copy in w_copies(k, second):
            copy.wait_recv()
        prepare_block(second)
        row_block(second)

    tops = top_s[...].T
    sums = sum_s[...].T
    top = jnp.max(tops, axis=0, keepdims=True)
    total = jnp.sum(sums * jnp.exp2(tops - top), axis=0, keepdims=True)
    nu_part = cbuf[0, 1:2]
    for b in range(1, nrow):
        nu_part = nu_part + cbuf[b, 1:2]
    nu_part = jnp.sum(nu_part, axis=1, keepdims=True)
    rowmsg[c, 0:1] = top
    rowmsg[c, 1:2] = total
    rowmsg[c, 2:3] = jnp.broadcast_to(nu_part, (1, rows))
    rowmsg[c, 3:4] = jnp.zeros((1, rows), F32)

    def rm_copy(k, owner):
        return to_col(rowmsg.at[owner], rowmsg.at[owner], rmsend.at[k], rmrecv.at[owner],
                      (c + k) % ncol)

    @pl.loop(1, ncol)
    def _(k):
        rm_copy(k, c).start()

    @pl.loop(1, ncol)
    def _(k):
        rm_copy(k, (c + ncol - k) % ncol).wait_recv()

    top = functools.reduce(jnp.maximum, [rowmsg[k, 0:1] for k in range(ncol)])
    total = sum(rowmsg[k, 1:2] * jnp.exp2(rowmsg[k, 0:1] - top) for k in range(ncol))
    nu_log = log2(sum(rowmsg[k, 2:3] for k in range(ncol)))
    f_row = nu_log - (top + log2(total))
    rowpot_ref[...] = (EPS * LN2) * f_row
    nu_col = jnp.broadcast_to(nu_log[:, 0:1], (1, cb))
    masses = jnp.concatenate([rbuf[k] for k in range(ncol)], axis=1)
    mu_part = jnp.broadcast_to(jnp.sum(masses, axis=1, keepdims=True), (1, cb))
    f_s[...] = rt_s[...] + jnp.broadcast_to(f_row, (128, rows)).T
    shifted = rt_s[...] + jnp.broadcast_to(f_row + log2(masses), (128, rows)).T
    put_rows(0, rows, shifted)

    def cm_copy(k, block, owner):
        return to_row(colout.at[block], colmsg.at[owner], cmsend.at[k], cmrecv.at[owner],
                      (r + k) % nrow)

    size = 64
    span_cols = min(512, cb)

    @pl.loop(0, nrow)
    def _(k):
        b = (r + 1 + k) % nrow
        put_cols(b, ct_s[b])
        dots(b)
        for span_start in range(0, cb, span_cols):
            span = slice(span_start, span_start + span_cols)
            lo = cb_s[b, :, span]

            def step(i, carry):
                old, total = carry
                vals = []
                for t in range(size // 8):
                    here = pl.ds(pl.multiple_of(i * size + t * 8, 8), 8)
                    rb = rb_s[here]
                    wide = jnp.concatenate([rb] * (span_cols // 128), axis=1)
                    vals.append(z_s[here, span] + jnp.maximum(lo, wide))
                top = functools.reduce(jnp.maximum, vals, old)
                total = total * jnp.exp2(old - top)
                for val in vals:
                    total = total + jnp.exp2(val - top)
                return top, total

            tops, sums = lax.fori_loop(
                0, rows // size, step,
                (jnp.full((8, span_cols), LOW, F32), jnp.zeros((8, span_cols), F32)),
                unroll=True)
            top = jnp.max(tops, axis=0, keepdims=True)
            colout[b, 0:1, span] = top
            colout[b, 1:2, span] = jnp.sum(sums * jnp.exp2(tops - top), axis=0, keepdims=True)
        colout[b, 2:3] = mu_part
        colout[b, 3:4] = jnp.zeros((1, cb), F32)

        @pl.when(k < nrow - 1)
        def _():
            cm_copy(k + 1, b, r).start()

    colmsg[r] = colout[r]
    put_rows(0, rows, f_s[...])

    @pl.loop(1, nrow)
    def _(k):
        cm_copy(k, r, (r + nrow - k) % nrow).wait_recv()

    top = functools.reduce(jnp.maximum, [colmsg[k, 0:1] for k in range(nrow)])
    total = sum(colmsg[k, 1:2] * jnp.exp2(colmsg[k, 0:1] - top) for k in range(nrow))
    mu_log = log2(sum(colmsg[k, 2:3] for k in range(nrow)))
    cpbuf[r] = (EPS * LN2) * (mu_log - (top + log2(total)))

    def cp_copy(k, owner):
        return to_row(cpbuf.at[owner], cpbuf.at[owner], cpsend.at[k], cprecv.at[owner],
                      (r + k) % nrow)

    @pl.loop(1, nrow)
    def _(k):
        cp_copy(k, r).start()

    g_s[...] = jnp.zeros(g_s.shape, F32)

    def g_copy(k, chunk_id, owner):
        return to_col(gout.at[chunk_id], gbuf.at[owner], gsend.at[k], grecv.at[owner],
                      (c + k) % ncol)

    def m_copy(k, chunk_id, owner):
        return to_col(mout.at[chunk_id], mbuf.at[owner], msend.at[k], mrecv.at[owner],
                      (c + k) % ncol)

    sub = min(256, cb)

    @pl.loop(0, ncol)
    def _(s):
        q = (c + ncol - 1 - s) % ncol
        base = pl.multiple_of(q * xs, xs)

        @pl.loop(0, nrow)
        def _(k):
            b = (r + nrow - k) % nrow

            @pl.when(s == 0)
            def _():
                @pl.when(k > 0)
                def _():
                    cp_copy(k, b).wait_recv()

                put_cols(b, ct_s[b] + (1.0 / (EPS * LN2)) * cpbuf[b]
                         + log2(cbuf[b, 1:2]) - nu_col)

            qq = q_s[pl.ds(base, xs)]
            acc = g_s[pl.ds(base, xs)]
            for start in range(0, cb, sub):
                cols = slice(start, start + sub)
                z = jnp.dot(qq, y_s[b, :, cols], preferred_element_type=F32)
                rb = rb_s[pl.ds(base, xs)]
                parts = []
                for t in range(0, sub, 128):
                    val = z[:, t:t + 128] + jnp.maximum(
                        cb_s[b, 0:1, start + t:start + t + 128], rb)
                    parts.append(jnp.exp2(val).astype(BF16))
                plan = jnp.concatenate(parts, axis=1)
                acc = acc + lax.dot_general(
                    plan, ft_s[b, :, cols], (((1,), (1,)), ((), ())),
                    preferred_element_type=F32)
            g_s[pl.ds(base, xs)] = acc

        gout[q] = g_s[pl.ds(base, xs), 0:128]
        mout[q] = g_s[pl.ds(base, xs), 128:256].T[0:8]

        @pl.when(s < ncol - 1)
        def _():
            g_copy(ncol - 1 - s, q, c).start()
            m_copy(ncol - 1 - s, q, c).start()

    for b in range(nrow):
        colpot_ref[b] = cpbuf[b]

    gbuf[c] = gout[c]
    mbuf[c] = mout[c]

    @pl.loop(1, ncol)
    def _(k):
        owner = (c + ncol - k) % ncol
        g_copy(k, c, owner).wait_recv()
        m_copy(k, c, owner).wait_recv()

    moments = sum(gbuf[k] for k in range(ncol))
    mass_row = sum(mbuf[k] for k in range(ncol))[0:1]
    mass = jnp.broadcast_to(mass_row, (128, xs)).T
    both = xm_ref[...].astype(F32)
    x = both[:, 0:128]
    h = both[:, 128:256]
    second = pltpu.roll(moments, 64, 1)
    grad = moments - x * mass
    curv = (second - 2.0 * x * moments + x * x * mass) / EPS + RIDGE
    new = h - damping_ref[...] * grad / curv
    mult_ref[...] = new[:, 0:width]

    @pl.loop(1, ncol)
    def _(k):
        x_copy(k, c).wait_send()
        r_copy(k, c).wait_send()
        rm_copy(k, c).wait_send()
        g_copy(k, (c + k) % ncol, c).wait_send()
        m_copy(k, (c + k) % ncol, c).wait_send()

    @pl.loop(1, nrow)
    def _(k):
        cm_copy(k, (r + k) % nrow, r).wait_send()
        cp_copy(k, r).wait_send()

    @pl.loop(0, half)
    def _(k):
        for copy in w_copies(k, same(k)):
            copy.wait_send()

    @pl.loop(1, half)
    def _(k):
        for copy in z_copies(k, r):
            copy.wait_send()


def on_device(nrow, ncol, x_points, y_points, row_mass, col_mass, multipliers, col_potential,
              basket, damping):
    xs, width = x_points.shape
    cb = y_points.shape[0]
    rows = xs * ncol
    xm = jnp.concatenate([x_points, x_points, multipliers, multipliers], axis=1)
    rmass = row_mass.astype(F32)[None, :]
    cmass = col_mass.astype(F32)
    cinfo = jnp.stack([SCALE * col_potential.astype(F32) + L2E * jnp.log(cmass), cmass])
    lanes = jnp.concatenate([basket, jnp.zeros((128 - width,), F32)])
    baskets = jnp.stack([jnp.broadcast_to(lanes[None, :], (128, 128)),
                         jnp.broadcast_to(lanes[:, None], (128, 128))])
    damp = jnp.concatenate([damping, damping])[None, :]
    half = nrow // 2
    dma = pltpu.SemaphoreType.DMA
    vmem = pltpu.VMEM
    whole = pl.BlockSpec(memory_space=pltpu.VMEM)
    row_pot, col_pot, mult = pl.pallas_call(
        functools.partial(kernel, nrow, ncol),
        out_shape=(jax.ShapeDtypeStruct((1, rows), F32),
                   jax.ShapeDtypeStruct((nrow, 1, cb), F32),
                   jax.ShapeDtypeStruct((xs, width), F32)),
        in_specs=[whole] * 6,
        out_specs=(whole,) * 3,
        scratch_shapes=[
            vmem((ncol, xs, 256), BF16), vmem((ncol, 1, xs), F32),
            vmem((nrow, width, cb), BF16), vmem((nrow, 2, cb), F32),
            vmem((ncol, 4, rows), F32), vmem((nrow, 4, cb), F32), vmem((nrow, 4, cb), F32),
            vmem((nrow, 1, cb), F32),
            vmem((ncol, xs, 128), F32), vmem((ncol, xs, 128), F32),
            vmem((ncol, 8, xs), F32), vmem((ncol, 8, xs), F32),
            vmem((rows, 256), BF16), vmem((rows, 128), F32), vmem((rows, 128), F32),
            vmem((rows, 128), F32), vmem((nrow, 256, cb), BF16), vmem((nrow, 256, cb), BF16),
            vmem((nrow, 8, cb), F32), vmem((nrow, 1, cb), F32),
            vmem((rows, 128), F32), vmem((rows, 128), F32), vmem((rows, cb), F32),
            vmem((8, 128), BF16), vmem((rows, 256), F32), vmem((rows, 128), F32),
            dma((ncol,)), dma((ncol,)), dma((ncol,)), dma((ncol,)),
            dma((half,)), dma((half,)), dma((nrow,)),
            dma((half,)), dma((half,)), dma((nrow,)),
            dma((ncol,)), dma((ncol,)), dma((nrow,)), dma((nrow,)),
            dma((nrow,)), dma((nrow,)), dma((ncol,)), dma((ncol,)),
            dma((ncol,)), dma((ncol,)),
        ],
        compiler_params=pltpu.CompilerParams(
            collective_id=0, has_side_effects=True, vmem_limit_bytes=56 * 1024 * 1024),
    )(xm, rmass, y_points.T, cinfo, baskets, damp)
    return row_pot.reshape(rows), col_pot.reshape(nrow * cb), mult


def solution(mesh):
    placed = (
        P(("row", "col"), None),
        P(("col", "row"), None),
        P(("row", "col")),
        P(("col", "row")),
        P(("row", "col"), None),
        P(("col", "row")),
        P(),
        P(),
    )
    return jax.shard_map(
        functools.partial(on_device, mesh.shape["row"], mesh.shape["col"]),
        mesh=mesh,
        in_specs=placed,
        out_specs=(P("row"), P("col"), P(("row", "col"), None)),
        check_vma=False,
    )
```

time: 509 us -> 84.3 us (0.17)
  blocking collectives: 195 us -> 0 us
  matrix products: 168 us -> 0 us
  Pallas kernels: 0 us -> 74.8 us
  loops' own time: 47.4 us -> 0 us
  other arithmetic: 28.6 us -> 3.22 us
  waiting for transfers between devices: 24.9 us -> 0 us
  local copies, waits for them, and re-layouts: 27.5 us -> 5.3 us
  between operations: 15.6 us -> 0.7 us
    dot_general x32 -> x0, matrix products: 168 us -> none  [the longest x24 163 us: scores(): lax.dot_general(query, y_float, (((1,), (1,)), ((), ())), precision=lax.P...]
    psum x3 -> x0, blocking collectives: 81.8 us -> none  [the longest x1 43.1 us: on_device(): lax.psum((jnp.sum(row_mass.astype(jnp.float32)), jnp.sum(col_mass.astype(...]
    all_gather x7 -> x0, blocking collectives: 80.4 us -> none  [the longest x1 26.1 us: on_device(): lax.all_gather(col_potential, 'row', axis=0, tiled=True)]
    pallas_call x0 -> x1, Pallas kernels: none -> 74.8 us  [on_device(): pl.pallas_call(functools.partial(kernel, nrow, ncol), out_shape=(jax.Shap...]
    another operation x4 -> x0, loops' own time: 47.4 us -> none  [the longest x1 15.8 us: on_device(): col_tops, col_totals = lax.map(col_pass, starts)]
    pmax x1 -> x0, blocking collectives: 33 us -> none  [on_device(): peak = lax.pmax(col_top, 'row')]
    psum x1 -> x0, waiting for transfers between devices: 24.9 us -> none  [on_device(): both_all, mass_all = lax.psum((both, mass), 'col')]
    reduce_sum x21 -> x0, other arithmetic: 20 us -> none  [the longest x8 6.03 us: row_pass(): total = jnp.sum(jnp.exp(z - top[:, None]), axis=1)]
  transfers between devices with their start and end apart: 2 -> 0, of which waited for: 1 -> 0; matrix products, arithmetic and copies ran while one was open for 1% -> 0% of each run, Pallas kernels for 0% -> 0%
where the time goes in v1:
time: 84.3 us; the launch traced here: 84 us
  Pallas kernels  74.8 us (89%)
  local copies, waits for them, and re-layouts  5.3 us (6%)
  other arithmetic  3.22 us (4%)
    pallas_call x1, Pallas kernels, on_device(): pl.pallas_call(functools.partial(kernel, nrow, ncol), out_shape=(jax.Shap...  74.8 us
    unnamed x23, local copies, waits for them, and re-layouts  5.22 us

profile of v1, /device:TPU:0, one launch (start us, length us, event | category | flops | bytes accessed | tf_op | source)
XLA Modules:
  0.0 84.0 jit_solution(9562860719725168775)
XLA Ops:
  0.6 0.0 copy-start.6
  0.6 0.6 copy-done.6
  1.3 0.0 copy-start.7
  1.3 0.0 copy-start.8
  1.3 0.6 copy-done.7
  1.9 0.0 copy-start.5
  1.9 0.6 maximum_bitcast_fusion.damping_ref
  2.5 0.0 copy-done.8
  2.5 0.0 copy-start.3
  2.5 0.6 broadcast_in_dim.14
  3.1 0.0 copy-done.5
  3.1 0.1 copy-done.3
  3.2 0.6 pad_maximum_fusion.2.cinfo_ref
  3.8 0.1 stack_broadcast_in_dim.5
  3.9 0.0 copy-start
  3.9 0.7 pad_maximum_fusion.1.basket_ref
  4.6 0.1 copy-done
  4.7 0.0 copy-start.1
  4.7 0.1 copy.11
  4.8 0.6 copy-done.1
  5.5 0.1 copy.13
  5.6 0.8 pad_maximum_fusion.xm_ref
  6.4 74.8 %shard_map.103 = (f32[1,1024]{1,0:T(1,128)}, f32[8,1,1024]{2,1,0:T(1,128)}, f32[256,64]{1,0:T(8,128)}) custom-call(bf16[256,256]{1,0:T(8,128)(2,1)} %pad_maximum_fusion.xm_ref, f32[1,256]{1,0:T(1,128)} %bitcast.13, bf16[64,1024]{1,0:T(8,128)(2,1)} %bitcast.8, f32[2,1024]{1,0:T(2,128)} %pad_maximum_fusion.2.cinfo_ref, ...), custom_call_target="tpu_custom_call" | custom-call | tf_op jit(solution)/shard_map/pallas_call | solution.py:449
  81.1 0.0 copy-start.4
  81.1 0.0 copy-start.2
  81.1 1.6 %copy.15 = f32[256,64]{0,1:T(8,128)} copy(f32[256,64]{1,0:T(8,128)} %get-tuple-element.11) | data formatting | bytes 131072
  82.8 0.0 copy-done.4
  82.8 0.6 copy.18
  83.4 0.0 copy-done.2
  83.4 0.6 copy.19
  (4 shorter events, 0.0 us)
Async XLA Ops:
  0.6 0.7 copy-start.6
  1.3 0.7 copy-start.7
  1.3 1.2 %copy-start.8 = (bf16[256]{0:T(256)(128)(2,1)S(1)}, bf16[256]{0:T(256)(128)(2,1)}, u32[]{:S(2)}) copy-start(bf16[256]{0:T(256)(128)(2,1)} %param.10) | copy-start | bytes 1540
  1.9 1.2 %copy-start.5 = (bf16[1024]{0:T(1024)(128)(2,1)S(1)}, bf16[1024]{0:T(1024)(128)(2,1)}, u32[]{:S(2)}) copy-start(bf16[1024]{0:T(1024)(128)(2,1)} %param.13) | copy-start | bytes 6148
  2.5 0.7 copy-start.3
  3.9 0.8 copy-start
  4.7 0.8 copy-start.1
  81.1 1.6 %copy-start.4 = (f32[1,1024]{1,0:T(1,128)S(1)}, f32[1,1024]{1,0:T(1,128)}, u32[]{:S(2)}) copy-start(f32[1,1024]{1,0:T(1,128)} %get-tuple-element.6) | copy-start | bytes 12292
  81.1 2.2 %copy-start.2 = (f32[8,1,1024]{2,1,0:T(1,128)S(1)}, f32[8,1,1024]{2,1,0:T(1,128)}, u32[]{:S(2)}) copy-start(f32[8,1,1024]{2,1,0:T(1,128)} %get-tuple-element.7) | copy-start | bytes 98308

commit v2 on v1

--- a/solution.py
+++ b/solution.py
@@ -31,16 +31,16 @@
 
 def kernel(
     nrow, ncol,
-    xm_ref, rmass_ref, yt_ref, cinfo_ref, basket_ref, damping_ref,
+    xt_ref, mt_ref, rmass_ref, yt_ref, pot_ref, cmass_ref, basket_ref, damping_ref,
     rowpot_ref, colpot_ref, mult_ref,
     xbuf, rbuf, ybuf, cbuf, rowmsg, colout, colmsg, cpbuf, gout, gbuf, mout, mbuf,
-    q_s, q3_s, rt_s, rb_s, y_s, ft_s, cb_s, ct_s, top_s, sum_s, z_s, plan_s, g_s, f_s,
+    q_s, q3_s, rt_s, rb_s, y_s, ft_s, cb_s, ct_s, top_s, sum_s, za_s, zb_s, bc_s, g_s, f_s,
     xsend, xrecv, rsend, rrecv, zsend, wsend, yrecv, czsend, cwsend, crecv,
     rmsend, rmrecv, cmsend, cmrecv, cpsend, cprecv, gsend, grecv, msend, mrecv,
 ):
     r = lax.axis_index("row")
     c = lax.axis_index("col")
-    xs = xm_ref.shape[0]
+    xs = xt_ref.shape[1]
     cb = yt_ref.shape[1]
     width = yt_ref.shape[0]
     rows = xs * ncol
@@ -71,10 +71,12 @@
         pl.semaphore_signal(barrier, inc=1, device_id=((r + k) % nrow, c),
                             device_id_type=pl.DeviceIdType.MESH)
 
-    xbuf[c] = xm_ref[...]
+    xbuf[c] = jnp.concatenate([xt_ref[...], mt_ref[...]], axis=0).astype(F32).T.astype(BF16)
     rbuf[c] = rmass_ref[...]
     ybuf[r] = yt_ref[...]
-    cbuf[r] = cinfo_ref[...]
+    cbuf[r, 0:1] = SCALE * pot_ref[...] + log2(cmass_ref[...])
+    cbuf[r, 1:2] = cmass_ref[...]
+    basket_row = jnp.concatenate([basket_ref[...], jnp.zeros((1, 128 - width), F32)], axis=1)
     pl.semaphore_wait(barrier, nrow + ncol - 2)
 
     def x_copy(k, owner):
@@ -91,7 +93,7 @@
         r_copy(k, c).start()
 
     def same(k):
-        return ((group + half - k) % half) * 2 + pair
+        return ((group + 2 * half - k) % half) * 2 + pair
 
     def other(k):
         return ((group + half - k) % half) * 2 + 1 - pair
@@ -112,6 +114,15 @@
     def _(k):
         for copy in z_copies(k, r):
             copy.start()
+
+    bc_s[...] = jnp.broadcast_to(basket_row, (128, 128)).T
+    one_lane = lax.broadcasted_iota(jnp.int32, (cb, 128), 1) == 0
+    ones = jnp.where(one_lane, 1.0, 0.0).astype(BF16)
+
+    @pl.loop(0, nrow)
+    def _(b):
+        y_s[b, 3 * width:4 * width] = jnp.zeros((width, cb), BF16)
+        ft_s[b, :, 128:256] = ones
 
     top_s[...] = jnp.full(top_s.shape, LOW, F32)
     sum_s[...] = jnp.zeros(sum_s.shape, F32)
@@ -123,14 +134,16 @@
         y_s[b, 0:width] = y16
         y_s[b, width:2 * width] = y16
         y_s[b, 2 * width:3 * width] = y16
-        y_s[b, 3 * width:4 * width] = jnp.zeros((width, cb), BF16)
-        ft_s[b, 0:width] = y16
-        ft_s[b, width:2 * width] = sq.astype(BF16)
-        ones = lax.broadcasted_iota(jnp.int32, (2 * width, cb), 0) == 0
-        ft_s[b, 2 * width:4 * width] = jnp.where(ones, 1.0, 0.0).astype(BF16)
+        ft_s[b, :, 0:128] = jnp.concatenate([yf, sq], axis=0).T.astype(BF16)
         ct_s[b] = -(SCALE * KAPPA / width) * jnp.sum(sq, axis=0, keepdims=True)
-        basket = SCALE * jnp.sum(yf * basket_ref[1][0:width, 0:1], axis=0, keepdims=True)
+        wide = jnp.concatenate([bc_s[0:width]] * (cb // 128), axis=1)
+        basket = SCALE * jnp.sum(yf * wide, axis=0, keepdims=True)
         cb_s[b] = jnp.broadcast_to(basket, (8, cb))
+
+    def doubled(both, lane):
+        both = both.astype(F32)
+        swapped = pltpu.roll(both, 64, 1)
+        return jnp.where(lane < 64, both, swapped), jnp.where(lane < 64, swapped, both)
 
     def put_cols(b, value):
         row = lax.broadcasted_iota(jnp.int32, (16, cb), 0)
@@ -160,13 +173,11 @@
 
     @pl.loop(0, ncol)
     def _(k):
-        both = xbuf[k].astype(F32)
-        x = both[:, 0:128]
-        h = both[:, 128:256]
         lane = lax.broadcasted_iota(jnp.int32, (xs, 128), 1)
+        x, h = doubled(xbuf[k], lane)
         one, two, three = split3(SCALE * (h + (2.0 * KAPPA / width) * x))
         here = pl.ds(k * xs, xs)
-        xb = x * basket_ref[0][0:1, :]
+        xb = x * basket_row
         q_s[here, 0:128] = jnp.where(lane < 64, one, two).astype(BF16)
         q3_s[here] = jnp.where(lane < 64, three, 0.0)
         term = -0.5 * (h * x + (KAPPA / width) * (x * x)) - xb
@@ -175,17 +186,19 @@
         rt_s[here] = rt
         put_rows(k * xs, xs, rt)
 
-    chunk = min(256, rows)
+    chunk = min(256, cb)
     tiles = cb // 128
 
-    def dots(b):
-        for start in range(0, rows, chunk):
-            z_s[start:start + chunk] = jnp.dot(
-                q_s[start:start + chunk], y_s[b], preferred_element_type=F32)
-
-    def row_block(b):
+    def dots(b, z_s):
+        for start in range(0, cb, chunk):
+            cols = slice(start, start + chunk)
+            z_s[:, cols] = jnp.dot(q_s[...], y_s[b, :, cols], preferred_element_type=F32)
+
+    def row_dots(b, z_s):
         put_cols(b, ct_s[b] + cbuf[b, 0:1])
-        dots(b)
+        dots(b, z_s)
+
+    def row_block(b, z_s):
         size = 32
 
         def step(i, _):
@@ -206,24 +219,29 @@
 
         lax.fori_loop(0, rows // size, step, 0, unroll=True)
 
+    row_dots(r, za_s)
+
     @pl.loop(0, half)
     def _(k):
         first = same(k)
-
-        @pl.when(k > 0)
-        def _():
-            for copy in z_copies(k, first):
-                copy.wait_recv()
-            for copy in w_copies(k, first):
-                copy.start()
-            prepare_block(first)
-
-        row_block(first)
         second = other(k)
         for copy in w_copies(k, second):
             copy.wait_recv()
         prepare_block(second)
-        row_block(second)
+        row_dots(second, zb_s)
+        row_block(first, za_s)
+        later = same(k + 1)
+
+        @pl.when(k < half - 1)
+        def _():
+            for copy in z_copies(k + 1, later):
+                copy.wait_recv()
+            for copy in w_copies(k + 1, later):
+                copy.start()
+            prepare_block(later)
+
+        row_dots(later, za_s)
+        row_block(second, zb_s)
 
     tops = top_s[...].T
     sums = sum_s[...].T
@@ -246,6 +264,10 @@
     def _(k):
         rm_copy(k, c).start()
 
+    masses = jnp.concatenate([rbuf[k] for k in range(ncol)], axis=1)
+    mu_part = jnp.broadcast_to(jnp.sum(masses, axis=1, keepdims=True), (1, cb))
+    top_s[...] = rt_s[...] + jnp.broadcast_to(log2(masses), (128, rows)).T
+
     @pl.loop(1, ncol)
     def _(k):
         rm_copy(k, (c + ncol - k) % ncol).wait_recv()
@@ -256,11 +278,9 @@
     f_row = nu_log - (top + log2(total))
     rowpot_ref[...] = (EPS * LN2) * f_row
     nu_col = jnp.broadcast_to(nu_log[:, 0:1], (1, cb))
-    masses = jnp.concatenate([rbuf[k] for k in range(ncol)], axis=1)
-    mu_part = jnp.broadcast_to(jnp.sum(masses, axis=1, keepdims=True), (1, cb))
-    f_s[...] = rt_s[...] + jnp.broadcast_to(f_row, (128, rows)).T
-    shifted = rt_s[...] + jnp.broadcast_to(f_row + log2(masses), (128, rows)).T
-    put_rows(0, rows, shifted)
+    f_col = jnp.broadcast_to(f_row, (128, rows)).T
+    f_s[...] = rt_s[...] + f_col
+    put_rows(0, rows, top_s[...] + f_col)
 
     def cm_copy(k, block, owner):
         return to_row(colout.at[block], colmsg.at[owner], cmsend.at[k], cmrecv.at[owner],
@@ -269,11 +289,13 @@
     size = 64
     span_cols = min(512, cb)
 
-    @pl.loop(0, nrow)
-    def _(k):
+    def col_dots(k, z_s):
         b = (r + 1 + k) % nrow
         put_cols(b, ct_s[b])
-        dots(b)
+        dots(b, z_s)
+
+    def col_block(k, z_s):
+        b = (r + 1 + k) % nrow
         for span_start in range(0, cb, span_cols):
             span = slice(span_start, span_start + span_cols)
             lo = cb_s[b, :, span]
@@ -306,6 +328,15 @@
         def _():
             cm_copy(k + 1, b, r).start()
 
+    col_dots(0, za_s)
+
+    @pl.loop(0, half)
+    def _(j):
+        col_dots(2 * j + 1, zb_s)
+        col_block(2 * j, za_s)
+        col_dots(2 * j + 2, za_s)
+        col_block(2 * j + 1, zb_s)
+
     colmsg[r] = colout[r]
     put_rows(0, rows, f_s[...])
 
@@ -338,40 +369,43 @@
 
     sub = min(256, cb)
 
+    def plan_of(b, qq, rb):
+        parts = []
+        for start in range(0, cb, sub):
+            z = jnp.dot(qq, y_s[b, :, start:start + sub], preferred_element_type=F32)
+            for t in range(0, sub, 128):
+                val = z[:, t:t + 128] + jnp.maximum(
+                    cb_s[b, 0:1, start + t:start + t + 128], rb)
+                parts.append(jnp.exp2(val).astype(BF16))
+        return jnp.concatenate(parts, axis=1)
+
     @pl.loop(0, ncol)
     def _(s):
         q = (c + ncol - 1 - s) % ncol
         base = pl.multiple_of(q * xs, xs)
 
-        @pl.loop(0, nrow)
-        def _(k):
-            b = (r + nrow - k) % nrow
+        @pl.loop(0, half)
+        def _(j):
+            first = (r + nrow - 2 * j) % nrow
+            second = (r + nrow - 2 * j - 1) % nrow
 
             @pl.when(s == 0)
             def _():
-                @pl.when(k > 0)
-                def _():
-                    cp_copy(k, b).wait_recv()
-
-                put_cols(b, ct_s[b] + (1.0 / (EPS * LN2)) * cpbuf[b]
-                         + log2(cbuf[b, 1:2]) - nu_col)
+                for k, b in ((2 * j, first), (2 * j + 1, second)):
+                    @pl.when(k > 0)
+                    def _():
+                        cp_copy(k, b).wait_recv()
+
+                    put_cols(b, ct_s[b] + (1.0 / (EPS * LN2)) * cpbuf[b]
+                             + log2(cbuf[b, 1:2]) - nu_col)
 
             qq = q_s[pl.ds(base, xs)]
-            acc = g_s[pl.ds(base, xs)]
-            for start in range(0, cb, sub):
-                cols = slice(start, start + sub)
-                z = jnp.dot(qq, y_s[b, :, cols], preferred_element_type=F32)
-                rb = rb_s[pl.ds(base, xs)]
-                parts = []
-                for t in range(0, sub, 128):
-                    val = z[:, t:t + 128] + jnp.maximum(
-                        cb_s[b, 0:1, start + t:start + t + 128], rb)
-                    parts.append(jnp.exp2(val).astype(BF16))
-                plan = jnp.concatenate(parts, axis=1)
-                acc = acc + lax.dot_general(
-                    plan, ft_s[b, :, cols], (((1,), (1,)), ((), ())),
-                    preferred_element_type=F32)
-            g_s[pl.ds(base, xs)] = acc
+            rb = rb_s[pl.ds(base, xs)]
+            plan_a = plan_of(first, qq, rb)
+            plan_b = plan_of(second, qq, rb)
+            g_s[pl.ds(base, xs)] += (
+                jnp.dot(plan_a, ft_s[first], preferred_element_type=F32)
+                + jnp.dot(plan_b, ft_s[second], preferred_element_type=F32))
 
         gout[q] = g_s[pl.ds(base, xs), 0:128]
         mout[q] = g_s[pl.ds(base, xs), 128:256].T[0:8]
@@ -396,14 +430,13 @@
     moments = sum(gbuf[k] for k in range(ncol))
     mass_row = sum(mbuf[k] for k in range(ncol))[0:1]
     mass = jnp.broadcast_to(mass_row, (128, xs)).T
-    both = xm_ref[...].astype(F32)
-    x = both[:, 0:128]
-    h = both[:, 128:256]
+    x, h = doubled(xbuf[c], lax.broadcasted_iota(jnp.int32, (xs, 128), 1))
     second = pltpu.roll(moments, 64, 1)
     grad = moments - x * mass
     curv = (second - 2.0 * x * moments + x * x * mass) / EPS + RIDGE
-    new = h - damping_ref[...] * grad / curv
-    mult_ref[...] = new[:, 0:width]
+    damping = jnp.concatenate([damping_ref[...], damping_ref[...]], axis=1)
+    new = h - damping * grad / curv
+    mult_ref[...] = new.T[0:width]
 
     @pl.loop(1, ncol)
     def _(k):
@@ -434,14 +467,9 @@
     xs, width = x_points.shape
     cb = y_points.shape[0]
     rows = xs * ncol
-    xm = jnp.concatenate([x_points, x_points, multipliers, multipliers], axis=1)
     rmass = row_mass.astype(F32)[None, :]
-    cmass = col_mass.astype(F32)
-    cinfo = jnp.stack([SCALE * col_potential.astype(F32) + L2E * jnp.log(cmass), cmass])
-    lanes = jnp.concatenate([basket, jnp.zeros((128 - width,), F32)])
-    baskets = jnp.stack([jnp.broadcast_to(lanes[None, :], (128, 128)),
-                         jnp.broadcast_to(lanes[:, None], (128, 128))])
-    damp = jnp.concatenate([damping, damping])[None, :]
+    cmass = col_mass.astype(F32)[None, :]
+    pot = col_potential.astype(F32)[None, :]
     half = nrow // 2
     dma = pltpu.SemaphoreType.DMA
     vmem = pltpu.VMEM
@@ -450,21 +478,21 @@
         functools.partial(kernel, nrow, ncol),
         out_shape=(jax.ShapeDtypeStruct((1, rows), F32),
                    jax.ShapeDtypeStruct((nrow, 1, cb), F32),
-                   jax.ShapeDtypeStruct((xs, width), F32)),
-        in_specs=[whole] * 6,
+                   jax.ShapeDtypeStruct((width, xs), F32)),
+        in_specs=[whole] * 8,
         out_specs=(whole,) * 3,
         scratch_shapes=[
-            vmem((ncol, xs, 256), BF16), vmem((ncol, 1, xs), F32),
+            vmem((ncol, xs, 128), BF16), vmem((ncol, 1, xs), F32),
             vmem((nrow, width, cb), BF16), vmem((nrow, 2, cb), F32),
             vmem((ncol, 4, rows), F32), vmem((nrow, 4, cb), F32), vmem((nrow, 4, cb), F32),
             vmem((nrow, 1, cb), F32),
             vmem((ncol, xs, 128), F32), vmem((ncol, xs, 128), F32),
             vmem((ncol, 8, xs), F32), vmem((ncol, 8, xs), F32),
             vmem((rows, 256), BF16), vmem((rows, 128), F32), vmem((rows, 128), F32),
-            vmem((rows, 128), F32), vmem((nrow, 256, cb), BF16), vmem((nrow, 256, cb), BF16),
+            vmem((rows, 128), F32), vmem((nrow, 256, cb), BF16), vmem((nrow, cb, 256), BF16),
             vmem((nrow, 8, cb), F32), vmem((nrow, 1, cb), F32),
             vmem((rows, 128), F32), vmem((rows, 128), F32), vmem((rows, cb), F32),
-            vmem((8, 128), BF16), vmem((rows, 256), F32), vmem((rows, 128), F32),
+            vmem((rows, cb), F32), vmem((128, 128), F32), vmem((rows, 256), F32), vmem((rows, 128), F32),
             dma((ncol,)), dma((ncol,)), dma((ncol,)), dma((ncol,)),
             dma((half,)), dma((half,)), dma((nrow,)),
             dma((half,)), dma((half,)), dma((nrow,)),
@@ -474,8 +502,8 @@
         ],
         compiler_params=pltpu.CompilerParams(
             collective_id=0, has_side_effects=True, vmem_limit_bytes=56 * 1024 * 1024),
-    )(xm, rmass, y_points.T, cinfo, baskets, damp)
-    return row_pot.reshape(rows), col_pot.reshape(nrow * cb), mult
+    )(x_points.T, multipliers.T, rmass, y_points.T, pot, cmass, basket[None, :], damping[None, :])
+    return row_pot.reshape(rows), col_pot.reshape(nrow * cb), mult.T
 
 
 def solution(mesh):

time: 84.3 us -> 86.7 us (1.028)
  Pallas kernels: 74.8 us -> 79.8 us
  other arithmetic: 3.22 us -> 1.75 us
  local copies, waits for them, and re-layouts: 5.3 us -> 4.17 us
    pallas_call x1, Pallas kernels: 74.8 us -> 79.8 us  [on_device(): pl.pallas_call(functools.partial(kernel, nrow, ncol), out_shape=(jax.Shap...]
    another operation x2 -> x0, other arithmetic: 1.28 us -> none  [the longest x1 0.66 us: on_device(): jnp.stack([jnp.broadcast_to(lanes[None, :], (128, 128)), jnp.broadcast_to...]
    unnamed x23 -> x11, local copies, waits for them, and re-layouts: 5.22 us -> 4.17 us
where the time goes in v2:
time: 86.7 us; the launch traced here: 86.4 us
  Pallas kernels  79.8 us (92%)
  local copies, waits for them, and re-layouts  4.17 us (5%)
  other arithmetic  1.75 us (2%)
    pallas_call x1, Pallas kernels, on_device(): pl.pallas_call(functools.partial(kernel, nrow, ncol), out_shape=(jax.Shap...  79.8 us
    unnamed x11, local copies, waits for them, and re-layouts  4.17 us

profile of v2, /device:TPU:0, one launch (start us, length us, event | category | flops | bytes accessed | tf_op | source)
XLA Modules:
  0.0 86.4 jit_solution(7429281663306356389)
XLA Ops:
  0.6 0.0 copy-start.3
  0.6 0.6 copy-done.3
  1.3 0.0 copy-start.1
  1.3 0.6 broadcast_in_dim.29
  1.9 0.1 copy-done.1
  2.0 0.0 copy-start.2
  2.0 0.6 broadcast_in_dim.31
  2.6 0.1 copy-done.2
  2.7 0.6 broadcast_in_dim.30
  3.3 79.8 %shard_map.103 = (f32[1,1024]{1,0:T(1,128)}, f32[8,1,1024]{2,1,0:T(1,128)}, f32[64,256]{1,0:T(8,128)}) custom-call(bf16[64,256]{1,0:T(8,128)(2,1)} %bitcast.13, bf16[64,256]{1,0:T(8,128)(2,1)} %bitcast.14, f32[1,256]{1,0:T(1,128)} %bitcast.19, bf16[64,1024]{1,0:T(8,128)(2,1)} %bitcast.11, f32[1,1024]{1,0:T(1,128)} %bitcast.17, f32[1,1024]{1,0:T(1,128)} %bitcast.16, ...), custom_call_target="tpu_custom_call" | custom-call | tf_op jit(solution)/shard_map/pallas_call | solution.py:477
  83.0 0.0 copy-start
  83.0 1.3 %copy.14 = f32[1024]{0:T(1024)} copy(f32[1024]{0:T(1024)} %bitcast.18) | data formatting | bytes 8192
  84.3 1.4 %copy.15 = f32[8192]{0:T(1024)} copy(f32[8192]{0:T(1024)} %bitcast.15) | data formatting | bytes 65536
  85.7 0.0 copy-done
  85.7 0.6 copy.16
Async XLA Ops:
  0.6 0.7 copy-start.3
  1.3 0.7 copy-start.1
  2.0 0.7 copy-start.2
  83.0 2.7 %copy-start = (f32[64,256]{1,0:T(8,128)S(1)}, f32[64,256]{1,0:T(8,128)}, u32[]{:S(2)}) copy-start(f32[64,256]{1,0:T(8,128)} %get-tuple-element.8) | copy-start | bytes 196612

commit v3 on v2

--- a/solution.py
+++ b/solution.py
@@ -116,13 +116,13 @@
             copy.start()
 
     bc_s[...] = jnp.broadcast_to(basket_row, (128, 128)).T
-    one_lane = lax.broadcasted_iota(jnp.int32, (cb, 128), 1) == 0
-    ones = jnp.where(one_lane, 1.0, 0.0).astype(BF16)
+    one_row = lax.broadcasted_iota(jnp.int32, (128, cb), 0) == 0
+    ones = jnp.where(one_row, 1.0, 0.0).astype(BF16)
 
     @pl.loop(0, nrow)
     def _(b):
         y_s[b, 3 * width:4 * width] = jnp.zeros((width, cb), BF16)
-        ft_s[b, :, 128:256] = ones
+        ft_s[b, 128:256] = ones
 
     top_s[...] = jnp.full(top_s.shape, LOW, F32)
     sum_s[...] = jnp.zeros(sum_s.shape, F32)
@@ -134,7 +134,8 @@
         y_s[b, 0:width] = y16
         y_s[b, width:2 * width] = y16
         y_s[b, 2 * width:3 * width] = y16
-        ft_s[b, :, 0:128] = jnp.concatenate([yf, sq], axis=0).T.astype(BF16)
+        ft_s[b, 0:width] = y16
+        ft_s[b, width:2 * width] = sq.astype(BF16)
         ct_s[b] = -(SCALE * KAPPA / width) * jnp.sum(sq, axis=0, keepdims=True)
         wide = jnp.concatenate([bc_s[0:width]] * (cb // 128), axis=1)
         basket = SCALE * jnp.sum(yf * wide, axis=0, keepdims=True)
@@ -189,59 +190,57 @@
     chunk = min(256, cb)
     tiles = cb // 128
 
-    def dots(b, z_s):
-        for start in range(0, cb, chunk):
-            cols = slice(start, start + chunk)
-            z_s[:, cols] = jnp.dot(q_s[...], y_s[b, :, cols], preferred_element_type=F32)
-
-    def row_dots(b, z_s):
+    row_chunk = min(256, rows)
+
+    def row_block(b):
         put_cols(b, ct_s[b] + cbuf[b, 0:1])
-        dots(b, z_s)
-
-    def row_block(b, z_s):
         size = 32
 
-        def step(i, _):
-            here = pl.ds(pl.multiple_of(i * size, size), size)
-            rb = rb_s[here]
-            vals = []
-            for t in range(tiles):
-                span = slice(t * 128, (t + 1) * 128)
-                vals.append(z_s[here, span] + jnp.maximum(cb_s[b, 0:1, span], rb))
-            old = top_s[here]
-            top = functools.reduce(jnp.maximum, vals, old)
-            total = sum_s[here] * jnp.exp2(old - top)
-            for val in vals:
-                total = total + jnp.exp2(val - top)
-            top_s[here] = top
-            sum_s[here] = total
-            return 0
-
-        lax.fori_loop(0, rows // size, step, 0, unroll=True)
-
-    row_dots(r, za_s)
+        def dots(start):
+            here = slice(start, start + row_chunk)
+            za_s[here] = jnp.dot(q_s[here], y_s[b], preferred_element_type=F32)
+
+        dots(0)
+        for start in range(0, rows, row_chunk):
+            if start + row_chunk < rows:
+                dots(start + row_chunk)
+
+            def step(i, _, start=start):
+                here = pl.ds(pl.multiple_of(start + i * size, size), size)
+                rb = rb_s[here]
+                vals = []
+                for t in range(tiles):
+                    span = slice(t * 128, (t + 1) * 128)
+                    vals.append(za_s[here, span] + jnp.maximum(cb_s[b, 0:1, span], rb))
+                old = top_s[here]
+                top = functools.reduce(jnp.maximum, vals, old)
+                total = sum_s[here] * jnp.exp2(old - top)
+                for val in vals:
+                    total = total + jnp.exp2(val - top)
+                top_s[here] = top
+                sum_s[here] = total
+                return 0
+
+            lax.fori_loop(0, row_chunk // size, step, 0, unroll=True)
 
     @pl.loop(0, half)
     def _(k):
         first = same(k)
+
+        @pl.when(k > 0)
+        def _():
+            for copy in z_copies(k, first):
+                copy.wait_recv()
+            for copy in w_copies(k, first):
+                copy.start()
+            prepare_block(first)
+
+        row_block(first)
         second = other(k)
         for copy in w_copies(k, second):
             copy.wait_recv()
         prepare_block(second)
-        row_dots(second, zb_s)
-        row_block(first, za_s)
-        later = same(k + 1)
-
-        @pl.when(k < half - 1)
-        def _():
-            for copy in z_copies(k + 1, later):
-                copy.wait_recv()
-            for copy in w_copies(k + 1, later):
-                copy.start()
-            prepare_block(later)
-
-        row_dots(later, za_s)
-        row_block(second, zb_s)
+        row_block(second)
 
     tops = top_s[...].T
     sums = sum_s[...].T
@@ -287,40 +286,46 @@
                       (r + k) % nrow)
 
     size = 64
-    span_cols = min(512, cb)
-
-    def col_dots(k, z_s):
+
+    def col_rows(k):
         b = (r + 1 + k) % nrow
         put_cols(b, ct_s[b])
-        dots(b, z_s)
-
-    def col_block(k, z_s):
+        return b
+
+    def col_dots(b, z_s, start):
+        cols = slice(start, start + chunk)
+        z_s[:, cols] = jnp.dot(q_s[...], y_s[b, :, cols], preferred_element_type=F32)
+
+    def col_part(b, z_s, start):
+        span = slice(start, start + chunk)
+        lo = cb_s[b, :, span]
+
+        def step(i, carry):
+            old, total = carry
+            vals = []
+            for t in range(size // 8):
+                here = pl.ds(pl.multiple_of(i * size + t * 8, 8), 8)
+                wide = jnp.concatenate([rb_s[here]] * (chunk // 128), axis=1)
+                vals.append(z_s[here, span] + jnp.maximum(lo, wide))
+            top = functools.reduce(jnp.maximum, vals, old)
+            total = total * jnp.exp2(old - top)
+            for val in vals:
+                total = total + jnp.exp2(val - top)
+            return top, total
+
+        tops, sums = lax.fori_loop(
+            0, rows // size, step,
+            (jnp.full((8, chunk), LOW, F32), jnp.zeros((8, chunk), F32)), unroll=True)
+        top = jnp.max(tops, axis=0, keepdims=True)
+        colout[b, 0:1, span] = top
+        colout[b, 1:2, span] = jnp.sum(sums * jnp.exp2(tops - top), axis=0, keepdims=True)
+
+    def col_turn(k, now, ahead):
         b = (r + 1 + k) % nrow
-        for span_start in range(0, cb, span_cols):
-            span = slice(span_start, span_start + span_cols)
-            lo = cb_s[b, :, span]
-
-            def step(i, carry):
-                old, total = carry
-                vals = []
-                for t in range(size // 8):
-                    here = pl.ds(pl.multiple_of(i * size + t * 8, 8), 8)
-                    rb = rb_s[here]
-                    wide = jnp.concatenate([rb] * (span_cols // 128), axis=1)
-                    vals.append(z_s[here, span] + jnp.maximum(lo, wide))
-                top = functools.reduce(jnp.maximum, vals, old)
-                total = total * jnp.exp2(old - top)
-                for val in vals:
-                    total = total + jnp.exp2(val - top)
-                return top, total
-
-            tops, sums = lax.fori_loop(
-                0, rows // size, step,
-                (jnp.full((8, span_cols), LOW, F32), jnp.zeros((8, span_cols), F32)),
-                unroll=True)
-            top = jnp.max(tops, axis=0, keepdims=True)
-            colout[b, 0:1, span] = top
-            colout[b, 1:2, span] = jnp.sum(sums * jnp.exp2(tops - top), axis=0, keepdims=True)
+        later = col_rows(k + 1)
+        for start in range(0, cb, chunk):
+            col_dots(later, ahead, start)
+            col_part(b, now, start)
         colout[b, 2:3] = mu_part
         colout[b, 3:4] = jnp.zeros((1, cb), F32)
 
@@ -328,14 +333,14 @@
         def _():
             cm_copy(k + 1, b, r).start()
 
-    col_dots(0, za_s)
+    start_block = col_rows(0)
+    for start in range(0, cb, chunk):
+        col_dots(start_block, za_s, start)
 
     @pl.loop(0, half)
     def _(j):
-        col_dots(2 * j + 1, zb_s)
-        col_block(2 * j, za_s)
-        col_dots(2 * j + 2, za_s)
-        col_block(2 * j + 1, zb_s)
+        col_turn(2 * j, za_s, zb_s)
+        col_turn(2 * j + 1, zb_s, za_s)
 
     colmsg[r] = colout[r]
     put_rows(0, rows, f_s[...])
@@ -368,6 +373,10 @@
                       (c + k) % ncol)
 
     sub = min(256, cb)
+
+    def moments_of(plan, b):
+        return lax.dot_general(plan, ft_s[b], (((1,), (1,)), ((), ())),
+                               preferred_element_type=F32)
 
     def plan_of(b, qq, rb):
         parts = []
@@ -404,8 +413,7 @@
             plan_a = plan_of(first, qq, rb)
             plan_b = plan_of(second, qq, rb)
             g_s[pl.ds(base, xs)] += (
-                jnp.dot(plan_a, ft_s[first], preferred_element_type=F32)
-                + jnp.dot(plan_b, ft_s[second], preferred_element_type=F32))
+                moments_of(plan_a, first) + moments_of(plan_b, second))
 
         gout[q] = g_s[pl.ds(base, xs), 0:128]
         mout[q] = g_s[pl.ds(base, xs), 128:256].T[0:8]
@@ -489,7 +497,7 @@
             vmem((ncol, xs, 128), F32), vmem((ncol, xs, 128), F32),
             vmem((ncol, 8, xs), F32), vmem((ncol, 8, xs), F32),
             vmem((rows, 256), BF16), vmem((rows, 128), F32), vmem((rows, 128), F32),
-            vmem((rows, 128), F32), vmem((nrow, 256, cb), BF16), vmem((nrow, cb, 256), BF16),
+            vmem((rows, 128), F32), vmem((nrow, 256, cb), BF16), vmem((nrow, 256, cb), BF16),
             vmem((nrow, 8, cb), F32), vmem((nrow, 1, cb), F32),
             vmem((rows, 128), F32), vmem((rows, 128), F32), vmem((rows, cb), F32),
             vmem((rows, cb), F32), vmem((128, 128), F32), vmem((rows, 256), F32), vmem((rows, 128), F32),

time: 86.7 us -> 83.8 us (0.967)
  Pallas kernels: 79.8 us -> 76.9 us
    pallas_call x1, Pallas kernels: 79.8 us -> 76.9 us  [on_device(): pl.pallas_call(functools.partial(kernel, nrow, ncol), out_shape=(jax.Shap...]
where the time goes in v3:
time: 83.8 us; the launch traced here: 83.5 us
  Pallas kernels  76.9 us (92%)
  local copies, waits for them, and re-layouts  4.17 us (5%)
  other arithmetic  1.75 us (2%)
    pallas_call x1, Pallas kernels, on_device(): pl.pallas_call(functools.partial(kernel, nrow, ncol), out_shape=(jax.Shap...  76.9 us
    unnamed x11, local copies, waits for them, and re-layouts  4.17 us

profile of v3, /device:TPU:0, one launch (start us, length us, event | category | flops | bytes accessed | tf_op | source)
XLA Modules:
  0.0 83.5 jit_solution(3329399578081558869)
XLA Ops:
  0.6 0.0 copy-start.3
  0.6 0.6 copy-done.3
  1.3 0.0 copy-start.1
  1.3 0.6 broadcast_in_dim.29
  1.9 0.1 copy-done.1
  2.0 0.0 copy-start.2
  2.0 0.6 broadcast_in_dim.31
  2.6 0.1 copy-done.2
  2.7 0.6 broadcast_in_dim.30
  3.3 76.9 %shard_map.103 = (f32[1,1024]{1,0:T(1,128)}, f32[8,1,1024]{2,1,0:T(1,128)}, f32[64,256]{1,0:T(8,128)}) custom-call(bf16[64,256]{1,0:T(8,128)(2,1)} %bitcast.13, bf16[64,256]{1,0:T(8,128)(2,1)} %bitcast.14, f32[1,256]{1,0:T(1,128)} %bitcast.19, bf16[64,1024]{1,0:T(8,128)(2,1)} %bitcast.11, f32[1,1024]{1,0:T(1,128)} %bitcast.17, f32[1,1024]{1,0:T(1,128)} %bitcast.16, ...), custom_call_target="tpu_custom_call" | custom-call | tf_op jit(solution)/shard_map/pallas_call | solution.py:485
  80.2 0.0 copy-start
  80.2 1.3 %copy.14 = f32[1024]{0:T(1024)} copy(f32[1024]{0:T(1024)} %bitcast.18) | data formatting | bytes 8192
  81.5 1.4 %copy.15 = f32[8192]{0:T(1024)} copy(f32[8192]{0:T(1024)} %bitcast.15) | data formatting | bytes 65536
  82.9 0.0 copy-done
  82.9 0.6 copy.16
Async XLA Ops:
  0.6 0.7 copy-start.3
  1.3 0.7 copy-start.1
  2.0 0.7 copy-start.2
  80.2 2.7 %copy-start = (f32[64,256]{1,0:T(8,128)S(1)}, f32[64,256]{1,0:T(8,128)}, u32[]{:S(2)}) copy-start(f32[64,256]{1,0:T(8,128)} %get-tuple-element.8) | copy-start | bytes 196612
